TPU v7x, 256 devices: a whole 4x4x8 slice. The times are simulated.
256 devices in a mesh: rows: 128 (over z, x, y), pair: 2 (over core).
Axes of the slice: x: 4, y: 4, z: 8, core: 2. Of those that a mesh axis runs over, the one named last changes fastest.
Arguments:
- a_blocks: bfloat16 [6144, 27, 4096], P(('rows', 'pair')), may hold values from -0.15625 to 0.15625
- a_cols: int32 [6144, 27], P(('rows', 'pair')), may hold values from 0 to 6143, as said below
- slots: int32 [6144, 27], P(('rows', 'pair')), may hold values from 0 to 7
- prolong: bfloat16 [6144, 4096], P(('rows', 'pair')), may hold values from -1.5 to 1.5
- aggregate: int32 [6144], P(('rows', 'pair')), may hold values from 0 to 511, as said below
- owner: int32 [32768, 1], P('rows'), may hold values from 0 to 127; in each aligned block of 256 rows (0 to 255, 256 to 511, ...) at most 4 rows name the same one
Outputs:
- agglomerated: float32 [128, 128, 4, 512], P('rows')
Inputs may be any that keep to these rules, and one draw needn't show every extreme that they name: a_cols[f, 0] = f, and a_cols[f, k] // 24 differs from f // 24 by at most one; the blocks of each existing neighbour (one at the first and last device) are named. aggregate[f] // 4 = f // 48; every coarse block is named. Among the 256 coarse rows of one chip, no owner is named by more than 4 rows, a bound that some block reaches.
All inputs are finite; a program needn't handle non-finite values.
Results may differ from a plain program's by a relative error of at most 0.0029.
Values may be sent and summed in bfloat16 or wider, within the bound.
A program may use at most 128 MiB of HBM per device.

v0:
```python
import jax
import jax.numpy as jnp
from jax import lax
from jax.sharding import PartitionSpec as P

BS = 64
KC = 8
CB_DEV = 4


def extended(cells, sides, width):
    for axis, dim in sides:
        count = lax.axis_size(axis)
        ends = count - 1
        head = lax.slice_in_dim(cells, 0, width, axis=dim)
        tail = lax.slice_in_dim(cells, cells.shape[dim] - width, cells.shape[dim], axis=dim)
        cells = jnp.concatenate(
            [
                lax.ppermute(tail, axis, [(i, (i + 1) % count) for i in range(ends)]),
                cells,
                lax.ppermute(head, axis, [((i + 1) % count, i) for i in range(ends)]),
            ],
            axis=dim,
        )
    return cells


def shards(a_blocks, a_cols, slots, prolong, aggregate, owner):
    highest = lax.Precision.HIGHEST
    fine_count = prolong.shape[0]
    block_size = BS
    list_length = a_blocks.shape[1]
    peer_count = lax.axis_size("rows")
    chip_index = lax.axis_index("rows")
    device = chip_index * lax.axis_size("pair") + lax.axis_index("pair")
    window = extended(prolong, ((("rows", "pair"), 0),), fine_count)
    local_cols = a_cols - (device - 1) * fine_count
    picked_flat = window[local_cols.reshape(-1)]
    picked = picked_flat.reshape(fine_count, list_length, block_size, block_size)
    blocks_square = a_blocks.reshape(fine_count, list_length, block_size, block_size)
    product = jnp.einsum(
        "fkij,fkjl->fkil", blocks_square, picked, preferred_element_type=jnp.float32
    )
    slot_onehot = (slots[..., None] == jnp.arange(KC, dtype=jnp.int32)).astype(jnp.float32)
    summed = jnp.einsum("fks,fkil->fsil", slot_onehot, product, precision=highest).astype(
        jnp.bfloat16
    )
    prolong_square = prolong.reshape(fine_count, block_size, block_size)
    galerkin = jnp.einsum(
        "fja,fsjb->fsab", prolong_square, summed, preferred_element_type=jnp.float32
    )
    member = (
        (aggregate - chip_index * CB_DEV)[:, None] == jnp.arange(CB_DEV, dtype=jnp.int32)
    ).astype(jnp.float32)
    row_count = CB_DEV * block_size
    coarse_parts = jnp.einsum("fc,fsab->csab", member, galerkin, precision=highest)
    pair_rows = jnp.transpose(coarse_parts, (0, 2, 1, 3)).reshape(row_count, KC * block_size)
    slot_count = 2 * row_count // peer_count
    dest_ids = owner[:, 0]
    target = (dest_ids[:, None] == jnp.arange(peer_count, dtype=jnp.int32)).astype(jnp.float32)
    earlier = (jnp.arange(row_count)[:, None] > jnp.arange(row_count)[None, :]).astype(jnp.float32)
    before = jnp.dot(earlier, target, precision=highest)
    rank_slot = jnp.sum(before * target, axis=1)
    placed = target[:, :, None] * (
        rank_slot[:, None, None] == jnp.arange(slot_count, dtype=jnp.float32)[None, None, :]
    ).astype(jnp.float32)
    chip_rows = lax.psum(pair_rows, "pair")
    arrived = lax.all_to_all(
        jnp.einsum("rdm,rx->dmx", placed, chip_rows, precision=highest),
        "rows",
        split_axis=0,
        concat_axis=0,
        tiled=True,
    )
    return arrived[None]


def solution(mesh):
    in_specs = (
        P(("rows", "pair"), None, None),
        P(("rows", "pair"), None),
        P(("rows", "pair"), None),
        P(("rows", "pair"), None),
        P(("rows", "pair")),
        P("rows", None),
    )
    out_specs = P("rows", None, None, None)
    return jax.shard_map(shards, mesh=mesh, in_specs=in_specs, out_specs=out_specs, check_vma=False)
```

profile of v0, /device:TPU:1, one launch (start us, length us, event | category | flops | bytes accessed | tf_op | source)
XLA Modules:
  0.0 212.7 jit_solution(11941403714582651531)
XLA Ops:
  6.5 0.0 all-reduce.2.cloned.1.call-start
  6.5 4.6 %collective-permute-start = (bf16[24,4096]{1,0:T(8,128)(2,1)}, bf16[24,4096]{1,0:T(8,128)(2,1)S(1)}, u32[]{:S(2)}, u32[]{:S(2)}) collective-permute-start(bf16[24,4096]{1,0:T(8,128)(2,1)} %param.9), channel_id=1, source_target_pairs={{0,1},{1,2},{2,3},{3,4},{4,5},{5,6},{6,7},{7,8},{8,9},{9,10},{10,1... | collective-permute-start | bytes 589832 | tf_op jit(solution)/shard_map/ppermute | solution.py:19
  11.1 1.9 collective-permute-start.1
  13.1 1.3 reshape.105
  14.4 0.7 broadcast_subtract_fusion
  15.1 0.1 reshape.91
  15.3 0.0 copy-start.3
  15.3 0.0 copy-start
  15.3 15.5 %reshape.93 = bf16[24,27,64,64]{3,2,0,1:T(8,128)(2,1)} reshape(bf16[24,27,4096]{2,0,1:T(8,128)(2,1)} %param.6) | data formatting | bytes 10616832 | tf_op jit(solution)/shard_map/reshape | solution.py:40
  30.8 0.0 copy-done.3
  30.8 0.0 collective-permute-done
  30.8 0.0 collective-permute-done.1
  30.8 0.0 copy-done
  30.8 5.5 %gather_fusion = bf16[648,4096]{1,0:T(8,128)(2,1)} fusion(bf16[72,4096]{1,0:T(8,128)(2,1)S(1)} %pad_maximum_fusion, s32[1024]{0:T(1024)S(1)} %pad_clamp_fusion), kind=kCustom, calls=%fused_computation | custom fusion | bytes 10619424 | tf_op jit(solution)/shard_map/gather | solution.py:38
  36.3 15.4 %reshape.92 = bf16[24,27,64,64]{3,2,1,0:T(8,128)(2,1)} reshape(bf16[648,4096]{1,0:T(8,128)(2,1)} %gather_fusion) | data formatting | bytes 10616832 | tf_op jit(solution)/shard_map/reshape | solution.py:39
  51.7 17.8 %fusion.2 = f32[24,27,64,64]{2,3,1,0:T(8,128)} fusion(bf16[24,27,64,64]{3,2,1,0:T(8,128)(2,1)} %reshape.92, bf16[24,27,64,64]{3,2,0,1:T(8,128)(2,1)} %reshape.93), kind=kOutput, calls=%fused_computation.3 | convolution fusion | flops 339738624 | bytes 21233664 | tf_op jit(solution)/shard_map/fkij,fkjl->fkil/dot_general | solution.py:41
  69.5 0.0 copy-start.1
  69.5 26.0 %copy.12 = f32[24,27,64,64]{3,1,2,0:T(8,128)} copy(f32[24,27,64,64]{2,3,1,0:T(8,128)} %fusion.2) | data formatting | bytes 21233664 | tf_op jit(solution)/shard_map/fkij,fkjl->fkil/dot_general | solution.py:41
  95.4 0.0 copy-done.1
  95.5 13.2 %convolution_convert_fusion = bf16[24,8,64,64]{3,1,2,0:T(8,128)(2,1)S(1)} fusion(f32[24,27,64,64]{3,1,2,0:T(8,128)} %copy.12, s32[24,27]{1,0:T(8,128)S(1)} %copy-done.1), kind=kOutput, calls=%fused_computation.7 | convolution fusion | flops 255595584 | bytes 12192288 | tf_op jit(solution)/shard_map/fks,fkil->fsil/dot_general | solution.py:45
  108.7 3.7 %fusion.7 = f32[24,8,64,64]{2,3,1,0:T(8,128)} fusion(bf16[24,8,64,64]{3,1,2,0:T(8,128)(2,1)S(1)} %convolution_convert_fusion, bf16[24,64,64,1]{2,1,0,3:T(8,128)(2,1)S(1)} %reshape.105), kind=kOutput, calls=%fused_computation.6 | convolution fusion | flops 100663296 | bytes 4915200 | tf_op jit(solution)/shard_map/fja,fsjb->fsab/dot_general | solution.py:49
  112.4 6.5 %copy.14 = f32[24,8,64,64]{3,0,2,1:T(8,128)} copy(f32[24,8,64,64]{2,3,1,0:T(8,128)} %fusion.7) | data formatting | bytes 6291456 | tf_op jit(solution)/shard_map/fja,fsjb->fsab/transpose | solution.py:49
  118.9 0.0 copy-start.2
  118.9 5.1 %convolution_bitcast_fusion = f32[4,64,8,64]{3,0,1,2:T(4,128)S(1)} fusion(f32[24,8,64,64]{3,0,2,1:T(8,128)} %copy.14, s32[24]{0:T(128)S(1)} %broadcast_subtract_fusion.1), kind=kOutput, calls=%fused_computation.8 | convolution fusion | flops 37748832 | bytes 3670112 | tf_op jit(solution)/shard_map/fc,fsab->csab/dot_general | solution.py:56
  124.0 0.6 copy.15
  124.7 1.1 reshape.95
  125.7 0.0 all-reduce.2.cloned.1.call-update
  125.7 0.0 copy-done.2
  125.8 0.2 fusion.10
  126.0 33.3 %all-reduce.2.cloned.1.call-done = f32[256,512]{1,0:T(8,128)} async-done(((f32[256,512]{1,0:T(8,128)}), f32[256,512]{1,0:T(8,128)}) %all-reduce.2.cloned.1.call-update) | async-done | bytes 524304 | tf_op jit(solution)/shard_map/psum | solution.py:67
  159.3 2.1 fusion.11
  161.4 0.7 copy.16
  162.1 42.8 %all_to_all.5 = f32[128,4,512]{2,1,0:T(4,128)S(1)} all-to-all(f32[128,4,512]{2,1,0:T(4,128)S(1)} %copy.16), channel_id=1, replica_groups=mesh['rows'=128,'pair'=2] {'rows'}, dimensions={0} | all-to-all | bytes 2097152 | tf_op jit(solution)/shard_map/all_to_all | solution.py:68
  204.8 1.0 copy.31
  (6 shorter events, 0.1 us)
Async XLA Ops:
  6.5 152.8 %all-reduce.2.cloned.1.call-start = ((), (), s32[]{:S(2)}) async-start(), calls=%async_computation.1 | async-start | bytes 1048576 | tf_op jit(solution)/shard_map/psum | solution.py:67
  6.5 24.2 %collective-permute-start = (bf16[24,4096]{1,0:T(8,128)(2,1)}, bf16[24,4096]{1,0:T(8,128)(2,1)S(1)}, u32[]{:S(2)}, u32[]{:S(2)}) collective-permute-start(bf16[24,4096]{1,0:T(8,128)(2,1)} %param.9), channel_id=1, source_target_pairs={{0,1},{1,2},{2,3},{3,4},{4,5},{5,6},{6,7},{7,8},{8,9},{9,10},{10,1... | collective-permute-start | bytes 589832 | tf_op jit(solution)/shard_map/ppermute | solution.py:19
  11.1 19.6 %collective-permute-start.1 = (bf16[24,4096]{1,0:T(8,128)(2,1)}, bf16[24,4096]{1,0:T(8,128)(2,1)S(1)}, u32[]{:S(2)}, u32[]{:S(2)}) collective-permute-start(bf16[24,4096]{1,0:T(8,128)(2,1)} %param.9), channel_id=1, source_target_pairs={{1,0},{2,1},{3,2},{4,3},{5,4},{6,5},{7,6},{8,7},{9,8},{10,9},{11,1... | collective-permute-start | bytes 589832 | tf_op jit(solution)/shard_map/ppermute | solution.py:21
  15.3 15.5 %copy-start.3 = (s32[24]{0:T(128)S(1)}, s32[24]{0:T(128)}, u32[]{:S(2)}) copy-start(s32[24]{0:T(128)} %param.10) | copy-start | bytes 292
  15.3 15.5 %copy-start = (bf16[24,4096]{1,0:T(8,128)(2,1)S(1)}, bf16[24,4096]{1,0:T(8,128)(2,1)}, u32[]{:S(2)}) copy-start(bf16[24,4096]{1,0:T(8,128)(2,1)} %param.9) | copy-start | bytes 589828
  69.5 26.0 %copy-start.1 = (s32[24,27]{1,0:T(8,128)S(1)}, s32[24,27]{1,0:T(8,128)}, u32[]{:S(2)}) copy-start(s32[24,27]{1,0:T(8,128)} %param.8) | copy-start | bytes 7780
  118.9 6.8 %copy-start.2 = (s32[256,1]{0,1:T(1,128)S(1)}, s32[256,1]{0,1:T(1,128)}, u32[]{:S(2)}) copy-start(s32[256,1]{0,1:T(1,128)} %param.11) | copy-start | bytes 3076
Sparse Core Ops, SparseCore 0:
  125.9 33.4 all-reduce.1
where the time goes:
time: 215 us; the launch traced here: 213 us
  local copies, waits for them, and re-layouts  73.7 us (34%)
  blocking collectives  42.8 us (20%)
  matrix products  42.1 us (20%)
  waiting for transfers between devices  33.3 us (15%)
  between operations  13.5 us (6%)
  starting transfers between devices  6.51 us (3%)
    all_to_all x1, blocking collectives, shards(): lax.all_to_all(jnp.einsum('rdm,rx->dmx', placed, chip_rows, precision=hig...  42.8 us
    psum x1, waiting for transfers between devices, shards(): chip_rows = lax.psum(pair_rows, 'pair')  33.3 us
    dot_general x1, local copies, waits for them, and re-layouts, shards(): jnp.einsum('fkij,fkjl->fkil', blocks_square, picked, preferred_element_ty...  26 us
    dot_general x1, matrix products, shards(): jnp.einsum('fkij,fkjl->fkil', blocks_square, picked, preferred_element_ty...  17.8 us
    reshape x1, local copies, waits for them, and re-layouts, shards(): a_blocks.reshape(fine_count, list_length, block_size, block_size)  15.5 us
    reshape x1, local copies, waits for them, and re-layouts, shards(): picked_flat.reshape(fine_count, list_length, block_size, block_size)  15.4 us
    dot_general x1, matrix products, shards(): jnp.einsum('fks,fkil->fsil', slot_onehot, product, precision=highest)  13.2 us
    transpose x1, local copies, waits for them, and re-layouts, shards(): jnp.einsum('fja,fsjb->fsab', prolong_square, summed, preferred_element_ty...  6.55 us
  transfers between devices with their start and end apart: 3, of which 1 were waited for; matrix products, arithmetic and copies ran while one was open for 8% of the time, Pallas kernels for 0%

commit v1 on v0

v1 whole, which is shorter than its diff:
```python
import functools

import jax
import jax.numpy as jnp
from jax import lax
from jax.experimental import pallas as pl
from jax.experimental.pallas import tpu as pltpu
from jax.sharding import PartitionSpec as P

BS = 64
KA = 27
KC = 8
FB = 24
CB = 4
MOST = 4
ROWS = CB * BS
COLS = KC * BS
HALF = COLS // 2
KT = 7
CHUNKS = 4
DIMS = (8, 4, 4)
MESH = pl.DeviceIdType.MESH
BF16 = jnp.bfloat16
F32 = jnp.float32


def kernel(
    dims,
    a_hbm,
    cols_ref,
    slots_ref,
    prolong_hbm,
    agg_ref,
    owner_ref,
    out_ref,
    a_ref,
    praw,
    stage,
    nat,
    left,
    window,
    masks,
    qperm,
    turned,
    summed,
    onehot,
    part,
    theirs,
    outbox,
    a_sem,
    p_sem,
    near_send,
    near_recv,
    pair_send,
    pair_recv,
    out_send,
    one_send,
    out_recv,
    fwd_send,
    fwd_recv,
    y_sem,
    x_sem,
):
    nz, nx, ny = dims
    chips = nz * nx * ny
    half = chips // 2
    chip = lax.axis_index("rows")
    core = lax.axis_index("pair")
    other = 1 - core
    z, x, y = chip // (nx * ny), (chip // ny) % nx, chip % ny
    beyond = (chip + chips - 1 + 2 * core) % chips

    per = FB // CHUNKS
    fetches = [
        pltpu.make_async_copy(
            a_hbm.at[pl.ds(i * per, per)], a_ref.at[pl.ds(i * per, per)], a_sem.at[i]
        )
        for i in range(CHUNKS)
    ]
    own = pltpu.make_async_copy(prolong_hbm, praw.at[1], p_sem)
    own.start()
    for fetch in fetches:
        fetch.start()

    y_ring = [(z * nx + x) * ny + (y + i) % ny for i in range(1, ny)]
    x_ring = [(z * nx + (x + i) % nx) * ny + y for i in range(1, nx)]
    z_ring = [(((z + i) % nz) * nx + x) * ny + y for i in range(1, nz)]
    barrier = pltpu.get_barrier_semaphore()
    met = [(chip, other), (beyond, other)] + [(c, core) for c in y_ring + x_ring + z_ring]
    for device in met:
        pl.semaphore_signal(barrier, inc=1, device_id=device, device_id_type=MESH)
    own.wait()
    pl.semaphore_wait(barrier, len(met))

    to_partner = pltpu.make_async_remote_copy(
        src_ref=praw.at[1],
        dst_ref=praw.at[2 * core],
        send_sem=near_send.at[0],
        recv_sem=near_recv.at[0],
        device_id=(chip, other),
        device_id_type=MESH,
    )
    to_beyond = pltpu.make_async_remote_copy(
        src_ref=praw.at[1],
        dst_ref=praw.at[2 * other],
        send_sem=near_send.at[1],
        recv_sem=near_recv.at[1],
        device_id=(beyond, other),
        device_id_type=MESH,
    )
    to_beyond.start()
    to_partner.start()
    for c in y_ring:
        pl.semaphore_signal(y_sem, inc=1, device_id=(c, core), device_id_type=MESH)

    lane = lax.broadcasted_iota(jnp.int32, (32, 128), 1)
    low = lane < BS

    column_slot = lax.broadcasted_iota(jnp.int32, (16, COLS), 1) // BS
    for s in range(KC):
        masks[s] = jnp.where(column_slot == s, 1.0, 0.0).astype(BF16)

    owner_col = owner_ref[...]
    owners = jnp.broadcast_to(owner_col, (ROWS, 128))
    target = jnp.where(
        owners == lax.broadcasted_iota(jnp.int32, (ROWS, 128), 1), 1.0, 0.0
    )
    earlier = jnp.where(
        lax.broadcasted_iota(jnp.int32, (ROWS, ROWS), 0)
        > lax.broadcasted_iota(jnp.int32, (ROWS, ROWS), 1),
        1.0,
        0.0,
    ).astype(BF16)
    before = jnp.dot(earlier, target.astype(BF16), preferred_element_type=F32)
    rank = jnp.sum(before * target, axis=1, keepdims=True)
    key = jnp.broadcast_to(owner_col.astype(F32) * MOST + rank, (ROWS, 128))
    key_row = jnp.transpose(key)[0:1, :]
    side = (chip // half + core) % 2
    row_id = lax.broadcasted_iota(jnp.int32, (256, ROWS), 0)
    for i in range(half * 16 // 256 if half >= 16 else 1):
        n = min(256, half * 16)
        rid = row_id[:n] + i * 256
        code = (side * half + rid // 16) * MOST + rid % MOST
        onehot[pl.ds(i * 256, n), :] = jnp.where(code.astype(F32) == key_row, 1.0, 0.0).astype(BF16)

    def relay_a(f, carry):
        for t in range(32):
            stage[pl.ds(t * 32, KA), :] = a_ref[f, :, pl.ds(t * 128, 128)].astype(F32)
        for g in range(14):
            one = stage[pl.ds(2 * g, 32, stride=32), :]
            if 2 * g + 1 < KA:
                two = stage[pl.ds(2 * g + 1, 32, stride=32), :]
            else:
                two = jnp.zeros_like(one)
            top = jnp.where(low, one, pltpu.roll(two, BS, 1))
            bottom = jnp.where(low, pltpu.roll(one, BS, 1), two)
            left[f, pl.ds(0, 32), pl.ds(g * 128, 128)] = top.astype(BF16)
            left[f, pl.ds(32, 32), pl.ds(g * 128, 128)] = bottom.astype(BF16)
        return carry

    def relay_p(w, keep):
        for t in range(32):
            stage[pl.ds(t * 32, FB), :] = praw[w, :, pl.ds(t * 128, 128)].astype(F32)

        def one_block(b, carry):
            one = stage[pl.ds(b, 32, stride=32), :]
            turn = pltpu.roll(one, BS, 1)
            top = jnp.where(low, one, turn)
            bottom = jnp.where(low, turn, one)
            if keep:
                qperm[pl.ds(pl.multiple_of(b * BS, BS), 32), :] = top
                qperm[pl.ds(pl.multiple_of(b * BS + 32, 32), 32), :] = bottom
            nat[pl.ds(0, 32, stride=2), :] = top
            nat[pl.ds(1, 32, stride=2), :] = bottom
            window[w * FB + b] = nat[...].astype(BF16)
            return carry

        lax.fori_loop(0, FB, one_block, 0)

    relay_p(1, True)
    wide = lax.broadcasted_iota(jnp.int32, (128, 128), 1) < BS
    tall = lax.broadcasted_iota(jnp.int32, (128, 128), 0) // BS
    for g in range(FB // 2):
        block = jnp.transpose(qperm[pl.ds(g * 128, 128), :])
        member = jnp.where(wide, agg_ref[2 * g], agg_ref[2 * g + 1]) - chip * CB
        for u in range(CB // 2):
            turned[pl.ds(u * 128, 128), pl.ds(g * 128, 128)] = jnp.where(
                member == tall + 2 * u, block, 0.0
            ).astype(BF16)

    for i in range(CHUNKS):
        fetches[i].wait()
        lax.fori_loop(i * per, (i + 1) * per, relay_a, 0)

    pl.semaphore_wait(y_sem, ny - 1)
    for c in x_ring:
        pl.semaphore_signal(x_sem, inc=1, device_id=(c, core), device_id_type=MESH)

    to_partner.wait_recv()
    relay_p(2 * other, False)
    to_beyond.wait_recv()
    relay_p(2 * core, False)

    base = (chip * 2 + core - 1) * FB
    pair_copies = []
    for h in range(2):

        def fine_row(f, carry):
            acc = jnp.zeros((BS, HALF), F32)
            for kk in range(KT):
                rows = []
                for k in range(4 * kk, 4 * kk + 4):
                    if k < KA:
                        block = window[jnp.clip(cols_ref[f, k] - base, 0, 3 * FB - 1)]
                        keep = masks[slots_ref[f, k], :, pl.ds(h * HALF, HALF)]
                        keep = jnp.concatenate([keep] * 4, axis=0)
                        rows.append(jnp.concatenate([block, block], axis=1) * keep)
                    else:
                        rows.append(jnp.zeros((BS, HALF), BF16))
                acc += jnp.dot(
                    left[f, :, pl.ds(kk * 256, 256)],
                    jnp.concatenate(rows, axis=0),
                    preferred_element_type=F32,
                )
            summed[pl.ds(pl.multiple_of(f * BS, BS), BS), pl.ds(h * HALF, HALF)] = acc.astype(BF16)
            return carry

        lax.fori_loop(0, FB, fine_row, 0)
        part[h] = jnp.dot(
            turned[...], summed[:, pl.ds(h * HALF, HALF)], preferred_element_type=F32
        )
        copy = pltpu.make_async_remote_copy(
            src_ref=part.at[h],
            dst_ref=theirs.at[h],
            send_sem=pair_send.at[h],
            recv_sem=pair_recv.at[h],
            device_id=(chip, other),
            device_id_type=MESH,
        )
        copy.start()
        pair_copies.append(copy)

    pl.semaphore_wait(x_sem, nx - 1)
    for copy in pair_copies:
        copy.wait()
    whole = jnp.concatenate(
        [(part[h] + theirs[h]).astype(BF16) for h in range(2)], axis=1
    )
    n = min(256, half * 16)
    group = (lax.broadcasted_iota(jnp.int32, (n, 128), 0) // MOST) % 4
    for i in range(half * 16 // n):
        placed = jnp.dot(onehot[pl.ds(i * n, n), :], whole, preferred_element_type=F32)
        value = placed[:, 384:512]
        for b in range(3):
            value = jnp.where(group == b, placed[:, b * 128 : (b + 1) * 128], value)
        for j in range(n // 16):
            outbox[i * (n // 16) + j] = value[j * 16 : (j + 1) * 16].astype(BF16)

    mine = chip % half

    def send(i, sem):
        there = (mine + i) % half
        return pltpu.make_async_remote_copy(
            src_ref=outbox.at[there],
            dst_ref=out_ref.at[chip],
            send_sem=sem,
            recv_sem=out_recv,
            device_id=(side * half + there, core),
            device_id_type=MESH,
        )

    def send_loop(i, carry):
        send(i, out_send).start()
        return carry

    lax.fori_loop(1, half, send_loop, 0)

    @pl.when(core == 0)
    def _():
        pltpu.make_async_copy(outbox.at[mine], out_ref.at[chip], out_recv).start()

    @pl.when(core == 1)
    def _():
        send(0, one_send).start()

    arrived = out_ref.at[pl.ds(side * half, half)]
    pltpu.make_async_copy(arrived, arrived, out_recv).wait()
    forward = pltpu.make_async_remote_copy(
        src_ref=arrived,
        dst_ref=arrived,
        send_sem=fwd_send,
        recv_sem=fwd_recv,
        device_id=(chip, other),
        device_id_type=MESH,
    )
    forward.start()
    sent = outbox.at[pl.ds(0, half - 1)]
    pltpu.make_async_copy(sent, sent, out_send).wait()

    @pl.when(core == 1)
    def _():
        send(0, one_send).wait_send()

    to_partner.wait_send()
    to_beyond.wait_send()
    forward.wait()


def shards(dims, a_blocks, a_cols, slots, prolong, aggregate, owner):
    chips = dims[0] * dims[1] * dims[2]
    half = chips // 2
    anywhere = pl.BlockSpec(memory_space=pl.ANY)
    vmem = pl.BlockSpec(memory_space=pltpu.VMEM)
    smem = pl.BlockSpec(memory_space=pltpu.SMEM)
    dma = pltpu.SemaphoreType.DMA
    arrived = pl.pallas_call(
        functools.partial(kernel, dims),
        out_shape=jax.ShapeDtypeStruct((chips, 16, 128), BF16),
        in_specs=[anywhere, smem, smem, anywhere, smem, vmem],
        out_specs=vmem,
        scratch_shapes=[
            pltpu.VMEM((FB, KA, BS * BS), BF16),
            pltpu.VMEM((3, FB, BS * BS), BF16),
            pltpu.VMEM((32 * 32, 128), F32),
            pltpu.VMEM((BS, 128), F32),
            pltpu.VMEM((FB, BS, KT * 256), BF16),
            pltpu.VMEM((3 * FB, BS, 128), BF16),
            pltpu.VMEM((KC, 16, COLS), BF16),
            pltpu.VMEM((FB * BS, 128), F32),
            pltpu.VMEM((ROWS, FB * BS), BF16),
            pltpu.VMEM((FB * BS, COLS), BF16),
            pltpu.VMEM((half * 16, ROWS), BF16),
            pltpu.VMEM((2, ROWS, HALF), F32),
            pltpu.VMEM((2, ROWS, HALF), F32),
            pltpu.VMEM((half, 16, 128), BF16),
            dma((CHUNKS,)),
            dma,
            dma((2,)),
            dma((2,)),
            dma((2,)),
            dma((2,)),
            dma,
            dma,
            dma,
            dma,
            dma,
            pltpu.SemaphoreType.REGULAR,
            pltpu.SemaphoreType.REGULAR,
        ],
        compiler_params=pltpu.CompilerParams(
            collective_id=0, has_side_effects=True, vmem_limit_bytes=48 * 1024 * 1024
        ),
    )(a_blocks, a_cols, slots, prolong, aggregate, owner)
    rows = arrived.reshape(chips, 4, MOST, 128).astype(F32)
    return jnp.transpose(rows, (0, 2, 1, 3)).reshape(1, chips, MOST, COLS)


def solution(mesh):
    in_specs = (
        P(("rows", "pair"), None, None),
        P(("rows", "pair"), None),
        P(("rows", "pair"), None),
        P(("rows", "pair"), None),
        P(("rows", "pair")),
        P("rows", None),
    )
    out_specs = P("rows", None, None, None)
    return jax.shard_map(
        functools.partial(shards, DIMS),
        mesh=mesh,
        in_specs=in_specs,
        out_specs=out_specs,
        check_vma=False,
    )
```

time: 215 us -> 67 us (0.31)
  the two profiles are of different devices: /device:TPU:1 before, /device:TPU:33 now
where the time goes in v1:
time: 67 us; the launch traced here: 66.9 us
  Pallas kernels  56.8 us (85%)
  local copies, waits for them, and re-layouts  9.01 us (13%)
  other arithmetic  1.05 us (2%)
    pallas_call x1, Pallas kernels, shards(): pl.pallas_call(functools.partial(kernel, dims), out_shape=jax.ShapeDtypeS...  56.8 us
    unnamed x10, local copies, waits for them, and re-layouts  9.01 us

profile of v1, /device:TPU:33, one launch (start us, length us, event | category | flops | bytes accessed | tf_op | source)
XLA Modules:
  0.0 66.9 jit_solution(393117377321652500)
XLA Ops:
  0.0 0.0 copy-start.3
  0.0 0.0 copy-start
  0.0 0.0 copy-start.2
  0.0 0.0 copy-start.1
  0.0 0.8 %copy.8.owner_ref = s32[256,1]{1,0:T(8,128)S(1)} copy(s32[256,1]{0,1:T(1,128)} %param.11) | data formatting | bytes 2048 | tf_op args[5]
  0.9 8.2 %copy.7.a_hbm = bf16[24,27,4096]{2,1,0:T(8,128)(2,1)} copy(bf16[24,27,4096]{2,0,1:T(8,128)(2,1)} %param.6) | data formatting | bytes 10616832 | tf_op args[0]
  9.0 0.0 copy-done.3
  9.0 0.0 copy-done
  9.0 0.0 copy-done.2
  9.0 0.0 copy-done.1
  9.0 56.8 %shard_map.64 = bf16[128,16,128]{2,1,0:T(8,128)(2,1)S(1)} custom-call(bf16[24,27,4096]{2,1,0:T(8,128)(2,1)} %copy.7.a_hbm, s32[24,27]{1,0:T(8,128)S(1)} %copy-done.1, s32[24,27]{1,0:T(8,128)S(1)} %copy-done.2, bf16[24,4096]{1,0:T(8,128)(2,1)S(1)} %copy-done, s32[24]{0:T(128)S(1)} %copy-done.3, s32[256,1]{1,0:T(8,128)S(1)} %copy.8.owner_ref), custom_call_target="tpu_custom_call" | custom-call | tf_op jit(solution)/shard_map/pallas_call | solution.py:316
  65.9 1.0 %convert.6 = f32[128,16,128]{2,1,0:T(8,128)} convert(bf16[128,16,128]{2,1,0:T(8,128)(2,1)S(1)} %shard_map.64) | non-fusion elementwise | flops 262144 | bytes 1572864
Async XLA Ops:
  0.0 9.0 %copy-start.3 = (s32[24]{0:T(128)S(1)}, s32[24]{0:T(128)}, u32[]{:S(2)}) copy-start(s32[24]{0:T(128)} %agg_ref.1) | copy-start | bytes 292
  0.0 9.0 %copy-start = (bf16[24,4096]{1,0:T(8,128)(2,1)S(1)}, bf16[24,4096]{1,0:T(8,128)(2,1)}, u32[]{:S(2)}) copy-start(bf16[24,4096]{1,0:T(8,128)(2,1)} %prolong_hbm.1) | copy-start | bytes 589828
  0.0 9.0 %copy-start.2 = (s32[24,27]{1,0:T(8,128)S(1)}, s32[24,27]{1,0:T(8,128)}, u32[]{:S(2)}) copy-start(s32[24,27]{1,0:T(8,128)} %slots_ref.1) | copy-start | bytes 7780
  0.0 9.0 %copy-start.1 = (s32[24,27]{1,0:T(8,128)S(1)}, s32[24,27]{1,0:T(8,128)}, u32[]{:S(2)}) copy-start(s32[24,27]{1,0:T(8,128)} %cols_ref.1) | copy-start | bytes 7780

commit v2 on v1

v2 whole, which is shorter than its diff:
```python
import functools

import jax
import jax.numpy as jnp
from jax import lax
from jax.experimental import pallas as pl
from jax.experimental.pallas import tpu as pltpu
from jax.sharding import PartitionSpec as P

BS = 64
KA = 27
KC = 8
FB = 24
CB = 4
MOST = 4
ROWS = CB * BS
COLS = KC * BS
HALF = COLS // 2
KT = 7
DIMS = (8, 4, 4)
MESH = pl.DeviceIdType.MESH
BF16 = jnp.bfloat16
F32 = jnp.float32


def fold_blocks(one, two, low):
    top = jnp.where(low, one, pltpu.roll(two, BS, 1))
    bottom = jnp.where(low, pltpu.roll(one, BS, 1), two)
    return top, bottom


def low_lanes():
    return lax.broadcasted_iota(jnp.int32, (32, 128), 1) < BS


def relay_a(g, a_ref, stage, left):
    low = low_lanes()
    for half in range(2):
        for t in range(32):
            stage[half, pl.ds(t * 32, FB), :] = a_ref[
                jnp.minimum(2 * g + half, KA - 1), :, pl.ds(t * 128, 128)
            ].astype(F32)
    column = pl.ds(pl.multiple_of(g * 128, 128), 128)
    for f in range(FB):
        one = stage[0, pl.ds(f, 32, stride=32), :]
        two = stage[1, pl.ds(f, 32, stride=32), :]
        top, bottom = fold_blocks(one, two, low)
        left[f, pl.ds(0, 32), column] = top.astype(BF16)
        left[f, pl.ds(32, 32), column] = bottom.astype(BF16)


def relay_p(w, keep, praw, stage, nat, window, qperm):
    low = low_lanes()
    for t in range(32):
        stage[0, pl.ds(t * 32, FB), :] = praw[w, :, pl.ds(t * 128, 128)].astype(F32)
    for b in range(FB):
        one = stage[0, pl.ds(b, 32, stride=32), :]
        top, bottom = fold_blocks(one, one, low)
        if keep:
            qperm[pl.ds(b * BS, 32), :] = top
            qperm[pl.ds(b * BS + 32, 32), :] = bottom
        nat[b % 4, pl.ds(0, 32, stride=2), :] = top
        nat[b % 4, pl.ds(1, 32, stride=2), :] = bottom
        window[w * FB + b] = nat[b % 4].astype(BF16)


def fill_masks(masks):
    column_slot = lax.broadcasted_iota(jnp.int32, (16, COLS), 1) // BS
    for s in range(KC):
        masks[s] = jnp.where(column_slot == s, 1.0, 0.0).astype(BF16)


def fill_onehot(side, half, owner_ref, onehot):
    owner_row = jnp.broadcast_to(owner_ref[...].astype(F32), (128, ROWS))
    owners = jnp.transpose(owner_row)
    target = jnp.where(
        owners == lax.broadcasted_iota(jnp.int32, (ROWS, 128), 1).astype(F32), 1.0, 0.0
    )
    earlier = jnp.where(
        lax.broadcasted_iota(jnp.int32, (ROWS, ROWS), 0)
        > lax.broadcasted_iota(jnp.int32, (ROWS, ROWS), 1),
        1.0,
        0.0,
    ).astype(BF16)
    before = jnp.dot(earlier, target.astype(BF16), preferred_element_type=F32)
    rank = jnp.sum(before * target, axis=1, keepdims=True)
    key_row = jnp.transpose(owners * MOST + rank)[0:1, :]
    n = min(256, half * 16)
    row_id = lax.broadcasted_iota(jnp.int32, (n, ROWS), 0)
    for i in range(half * 16 // n):
        rid = row_id + i * n
        code = (side * half + rid // 16) * MOST + rid % MOST
        onehot[pl.ds(i * n, n), :] = jnp.where(code.astype(F32) == key_row, 1.0, 0.0).astype(BF16)


def fill_turned(chip, agg_ref, qperm, turned):
    wide = lax.broadcasted_iota(jnp.int32, (128, 128), 1) < BS
    tall = lax.broadcasted_iota(jnp.int32, (128, 128), 0) // BS
    for g in range(FB // 2):
        block = jnp.transpose(qperm[pl.ds(g * 128, 128), :])
        member = jnp.where(wide, agg_ref[2 * g], agg_ref[2 * g + 1]) - chip * CB
        for u in range(CB // 2):
            turned[pl.ds(u * 128, 128), pl.ds(g * 128, 128)] = jnp.where(
                member == tall + 2 * u, block, 0.0
            ).astype(BF16)


def fine_row(f, h, base, cols_ref, slots_ref, left, window, masks, summed):
    acc = jnp.zeros((BS, HALF), F32)
    for kk in range(KT):
        rows = []
        for k in range(4 * kk, 4 * kk + 4):
            if k < KA:
                block = window[jnp.clip(cols_ref[f, k] - base, 0, 3 * FB - 1)]
                keep = masks[slots_ref[f, k], :, pl.ds(h * HALF, HALF)]
                keep = jnp.concatenate([keep] * 4, axis=0)
                rows.append(jnp.concatenate([block, block], axis=1) * keep)
            else:
                rows.append(jnp.zeros((BS, HALF), BF16))
        acc += jnp.dot(
            left[f, :, pl.ds(kk * 256, 256)],
            jnp.concatenate(rows, axis=0),
            preferred_element_type=F32,
        )
    summed[pl.ds(pl.multiple_of(f * BS, BS), BS), pl.ds(h * HALF, HALF)] = acc.astype(BF16)


def place(half, onehot, part, theirs, outbox):
    whole = jnp.concatenate([(part[h] + theirs[h]).astype(BF16) for h in range(2)], axis=1)
    n = min(256, half * 16)
    group = (lax.broadcasted_iota(jnp.int32, (n, 128), 0) // MOST) % 4
    for i in range(half * 16 // n):
        placed = jnp.dot(onehot[pl.ds(i * n, n), :], whole, preferred_element_type=F32)
        value = placed[:, 384:512]
        for b in range(3):
            value = jnp.where(group == b, placed[:, b * 128 : (b + 1) * 128], value)
        for j in range(n // 16):
            outbox[i * (n // 16) + j] = value[j * 16 : (j + 1) * 16].astype(BF16)


def kernel(
    dims,
    a_hbm,
    cols_ref,
    slots_ref,
    prolong_hbm,
    agg_ref,
    owner_ref,
    out_ref,
    a_ref,
    praw,
    stage,
    nat,
    left,
    window,
    masks,
    qperm,
    turned,
    summed,
    onehot,
    part,
    theirs,
    outbox,
    a_sem,
    p_sem,
    near_send,
    near_recv,
    pair_send,
    pair_recv,
    out_send,
    one_send,
    out_recv,
    fwd_send,
    fwd_recv,
    y_sem,
    x_sem,
):
    nz, nx, ny = dims
    chips = nz * nx * ny
    half = chips // 2
    chip = lax.axis_index("rows")
    core = lax.axis_index("pair")
    other = 1 - core
    z, x, y = chip // (nx * ny), (chip // ny) % nx, chip % ny
    beyond = (chip + chips - 1 + 2 * core) % chips

    fetches = []
    for i in range(KT):
        span = pl.ds(4 * i, min(4, KA - 4 * i))
        fetches.append(pltpu.make_async_copy(a_hbm.at[span], a_ref.at[span], a_sem.at[i]))
    own = pltpu.make_async_copy(prolong_hbm, praw.at[1], p_sem)
    own.start()
    for fetch in fetches:
        fetch.start()

    y_ring = [(z * nx + x) * ny + (y + i) % ny for i in range(1, ny)]
    x_ring = [(z * nx + (x + i) % nx) * ny + y for i in range(1, nx)]
    z_ring = [(((z + i) % nz) * nx + x) * ny + y for i in range(1, nz)]
    barrier = pltpu.get_barrier_semaphore()
    met = [(chip, other), (beyond, other)] + [(c, core) for c in y_ring + x_ring + z_ring]
    for device in met:
        pl.semaphore_signal(barrier, inc=1, device_id=device, device_id_type=MESH)
    own.wait()
    pl.semaphore_wait(barrier, len(met))

    to_partner = pltpu.make_async_remote_copy(
        src_ref=praw.at[1],
        dst_ref=praw.at[2 * core],
        send_sem=near_send.at[0],
        recv_sem=near_recv.at[0],
        device_id=(chip, other),
        device_id_type=MESH,
    )
    to_beyond = pltpu.make_async_remote_copy(
        src_ref=praw.at[1],
        dst_ref=praw.at[2 * other],
        send_sem=near_send.at[1],
        recv_sem=near_recv.at[1],
        device_id=(beyond, other),
        device_id_type=MESH,
    )
    to_beyond.start()
    to_partner.start()
    for c in y_ring:
        pl.semaphore_signal(y_sem, inc=1, device_id=(c, core), device_id_type=MESH)

    side = (chip // half + core) % 2
    fill_masks(masks)
    fill_onehot(side, half, owner_ref, onehot)
    relay_p(1, True, praw, stage, nat, window, qperm)
    fill_turned(chip, agg_ref, qperm, turned)

    for i in range(KT):
        fetches[i].wait()

        def relay(g, carry):
            relay_a(g, a_ref, stage, left)
            return carry

        lax.fori_loop(2 * i, 2 * i + 2, relay, 0)

    pl.semaphore_wait(y_sem, ny - 1)
    for c in x_ring:
        pl.semaphore_signal(x_sem, inc=1, device_id=(c, core), device_id_type=MESH)

    to_partner.wait_recv()
    relay_p(2 * other, False, praw, stage, nat, window, qperm)
    to_beyond.wait_recv()
    relay_p(2 * core, False, praw, stage, nat, window, qperm)

    base = (chip * 2 + core - 1) * FB
    pair_copies = []
    for h in range(2):

        def row(f, carry):
            fine_row(f, h, base, cols_ref, slots_ref, left, window, masks, summed)
            return carry

        lax.fori_loop(0, FB, row, 0)
        part[h] = jnp.dot(
            turned[...], summed[:, pl.ds(h * HALF, HALF)], preferred_element_type=F32
        )
        copy = pltpu.make_async_remote_copy(
            src_ref=part.at[h],
            dst_ref=theirs.at[h],
            send_sem=pair_send.at[h],
            recv_sem=pair_recv.at[h],
            device_id=(chip, other),
            device_id_type=MESH,
        )
        copy.start()
        pair_copies.append(copy)

    pl.semaphore_wait(x_sem, nx - 1)
    for copy in pair_copies:
        copy.wait()
    place(half, onehot, part, theirs, outbox)

    mine = chip % half

    def send(i, sem):
        there = (mine + i) % half
        return pltpu.make_async_remote_copy(
            src_ref=outbox.at[there],
            dst_ref=out_ref.at[chip],
            send_sem=sem,
            recv_sem=out_recv,
            device_id=(side * half + there, core),
            device_id_type=MESH,
        )

    def send_loop(i, carry):
        send(i, out_send).start()
        return carry

    lax.fori_loop(1, half, send_loop, 0)

    @pl.when(core == 0)
    def _():
        pltpu.make_async_copy(outbox.at[mine], out_ref.at[chip], out_recv).start()

    @pl.when(core == 1)
    def _():
        send(0, one_send).start()

    arrived = out_ref.at[pl.ds(side * half, half)]
    pltpu.make_async_copy(arrived, arrived, out_recv).wait()
    forward = pltpu.make_async_remote_copy(
        src_ref=arrived,
        dst_ref=arrived,
        send_sem=fwd_send,
        recv_sem=fwd_recv,
        device_id=(chip, other),
        device_id_type=MESH,
    )
    forward.start()
    sent = outbox.at[pl.ds(0, half - 1)]
    pltpu.make_async_copy(sent, sent, out_send).wait()

    @pl.when(core == 1)
    def _():
        send(0, one_send).wait_send()

    to_partner.wait_send()
    to_beyond.wait_send()
    forward.wait()


def shards(dims, a_blocks, a_cols, slots, prolong, aggregate, owner):
    chips = dims[0] * dims[1] * dims[2]
    half = chips // 2
    anywhere = pl.BlockSpec(memory_space=pl.ANY)
    vmem = pl.BlockSpec(memory_space=pltpu.VMEM)
    smem = pl.BlockSpec(memory_space=pltpu.SMEM)
    dma = pltpu.SemaphoreType.DMA
    arrived = pl.pallas_call(
        functools.partial(kernel, dims),
        out_shape=jax.ShapeDtypeStruct((chips, 16, 128), BF16),
        in_specs=[anywhere, smem, smem, anywhere, smem, vmem],
        out_specs=vmem,
        scratch_shapes=[
            pltpu.VMEM((KA, FB, BS * BS), BF16),
            pltpu.VMEM((3, FB, BS * BS), BF16),
            pltpu.VMEM((2, 32 * 32, 128), F32),
            pltpu.VMEM((4, BS, 128), F32),
            pltpu.VMEM((FB, BS, KT * 256), BF16),
            pltpu.VMEM((3 * FB, BS, 128), BF16),
            pltpu.VMEM((KC, 16, COLS), BF16),
            pltpu.VMEM((FB * BS, 128), F32),
            pltpu.VMEM((ROWS, FB * BS), BF16),
            pltpu.VMEM((FB * BS, COLS), BF16),
            pltpu.VMEM((half * 16, ROWS), BF16),
            pltpu.VMEM((2, ROWS, HALF), F32),
            pltpu.VMEM((2, ROWS, HALF), F32),
            pltpu.VMEM((half, 16, 128), BF16),
            dma((KT,)),
            dma,
            dma((2,)),
            dma((2,)),
            dma((2,)),
            dma((2,)),
            dma,
            dma,
            dma,
            dma,
            dma,
            pltpu.SemaphoreType.REGULAR,
            pltpu.SemaphoreType.REGULAR,
        ],
        compiler_params=pltpu.CompilerParams(
            collective_id=0, has_side_effects=True, vmem_limit_bytes=48 * 1024 * 1024
        ),
    )(
        jnp.transpose(a_blocks, (1, 0, 2)),
        a_cols,
        slots,
        prolong,
        aggregate,
        owner.reshape(1, ROWS),
    )
    rows = arrived.reshape(chips, 4, MOST, 128).astype(F32)
    return jnp.transpose(rows, (0, 2, 1, 3)).reshape(1, chips, MOST, COLS)


def solution(mesh):
    in_specs = (
        P(("rows", "pair"), None, None),
        P(("rows", "pair"), None),
        P(("rows", "pair"), None),
        P(("rows", "pair"), None),
        P(("rows", "pair")),
        P("rows", None),
    )
    out_specs = P("rows", None, None, None)
    return jax.shard_map(
        functools.partial(shards, DIMS),
        mesh=mesh,
        in_specs=in_specs,
        out_specs=out_specs,
        check_vma=False,
    )
```

time: 67 us -> 59.2 us (0.88)
  Pallas kernels: 56.8 us -> 51.7 us
  local copies, waits for them, and re-layouts: 9.01 us -> 6.18 us
    pallas_call x1, Pallas kernels: 56.8 us -> 51.7 us  [shards(): pl.pallas_call(functools.partial(kernel, dims), out_shape=jax.ShapeDtypeS...]
    unnamed x10 -> x12, local copies, waits for them, and re-layouts: 9.01 us -> 6.18 us
where the time goes in v2:
time: 59.2 us; the launch traced here: 59 us
  Pallas kernels  51.7 us (87%)
  local copies, waits for them, and re-layouts  6.18 us (10%)
  other arithmetic  1.05 us (2%)
    pallas_call x1, Pallas kernels, shards(): pl.pallas_call(functools.partial(kernel, dims), out_shape=jax.ShapeDtypeS...  51.7 us
    unnamed x12, local copies, waits for them, and re-layouts  6.18 us

profile of v2, /device:TPU:33, one launch (start us, length us, event | category | flops | bytes accessed | tf_op | source)
XLA Modules:
  0.0 59.0 jit_solution(2648011874466647479)
XLA Ops:
  0.0 0.0 copy-start
  0.0 2.5 %copy-done = bf16[24,27,4096]{2,0,1:T(8,128)(2,1)S(1)} copy-done((bf16[24,27,4096]{2,0,1:T(8,128)(2,1)S(1)}, bf16[24,27,4096]{2,0,1:T(8,128)(2,1)}, u32[]{:S(2)}) %copy-start) | copy-done | bytes 5308440
  2.5 0.0 copy-start.1
  2.5 0.9 %copy-done.1 = bf16[24,4096]{1,0:T(8,128)(2,1)S(1)} copy-done((bf16[24,4096]{1,0:T(8,128)(2,1)S(1)}, bf16[24,4096]{1,0:T(8,128)(2,1)}, u32[]{:S(2)}) %copy-start.1) | copy-done | bytes 196632
  3.4 0.0 copy-start.2
  3.4 0.7 %copy-done.2 = s32[24,27]{1,0:T(8,128)S(1)} copy-done((s32[24,27]{1,0:T(8,128)S(1)}, s32[24,27]{1,0:T(8,128)}, u32[]{:S(2)}) %copy-start.2) | copy-done | bytes 2616
  4.1 0.0 copy-start.3
  4.1 0.7 %copy-done.3 = s32[24,27]{1,0:T(8,128)S(1)} copy-done((s32[24,27]{1,0:T(8,128)S(1)}, s32[24,27]{1,0:T(8,128)}, u32[]{:S(2)}) %copy-start.3) | copy-done | bytes 2616
  4.8 0.0 copy-start.4
  4.8 0.7 %copy-done.4 = s32[256,1]{0,1:T(1,128)S(1)} copy-done((s32[256,1]{0,1:T(1,128)S(1)}, s32[256,1]{0,1:T(1,128)}, u32[]{:S(2)}) %copy-start.4) | copy-done | bytes 1048
  5.5 0.0 copy-start.5
  5.5 0.7 %copy-done.5 = s32[24]{0:T(128)S(1)} copy-done((s32[24]{0:T(128)S(1)}, s32[24]{0:T(128)}, u32[]{:S(2)}) %copy-start.5) | copy-done | bytes 120
  6.2 51.7 %shard_map.64 = bf16[128,16,128]{2,1,0:T(8,128)(2,1)S(1)} custom-call(bf16[27,24,4096]{2,1,0:T(8,128)(2,1)S(1)} %bitcast.10, s32[24,27]{1,0:T(8,128)S(1)} %copy-done.2, s32[24,27]{1,0:T(8,128)S(1)} %copy-done.3, bf16[24,4096]{1,0:T(8,128)(2,1)S(1)} %copy-done.1, s32[24]{0:T(128)S(1)} %copy-done.5, s32[1,256]{1,0:T(1,128)S(1)} %bitcast.11), custom_call_target="tpu_custom_call" | custom-call | tf_op jit(solution)/shard_map/pallas_call | solution.py:336
  57.9 1.0 %convert.6 = f32[128,16,128]{2,1,0:T(8,128)} convert(bf16[128,16,128]{2,1,0:T(8,128)(2,1)S(1)} %shard_map.64) | non-fusion elementwise | flops 262144 | bytes 1572864
Async XLA Ops:
  0.0 2.5 %copy-start = (bf16[24,27,4096]{2,0,1:T(8,128)(2,1)S(1)}, bf16[24,27,4096]{2,0,1:T(8,128)(2,1)}, u32[]{:S(2)}) copy-start(bf16[24,27,4096]{2,0,1:T(8,128)(2,1)} %param.6) | copy-start | bytes 15925252
  2.5 0.9 %copy-start.1 = (bf16[24,4096]{1,0:T(8,128)(2,1)S(1)}, bf16[24,4096]{1,0:T(8,128)(2,1)}, u32[]{:S(2)}) copy-start(bf16[24,4096]{1,0:T(8,128)(2,1)} %prolong_hbm.1) | copy-start | bytes 589828
  3.4 0.7 %copy-start.2 = (s32[24,27]{1,0:T(8,128)S(1)}, s32[24,27]{1,0:T(8,128)}, u32[]{:S(2)}) copy-start(s32[24,27]{1,0:T(8,128)} %cols_ref.1) | copy-start | bytes 7780
  4.1 0.7 %copy-start.3 = (s32[24,27]{1,0:T(8,128)S(1)}, s32[24,27]{1,0:T(8,128)}, u32[]{:S(2)}) copy-start(s32[24,27]{1,0:T(8,128)} %slots_ref.1) | copy-start | bytes 7780
  4.8 0.7 %copy-start.4 = (s32[256,1]{0,1:T(1,128)S(1)}, s32[256,1]{0,1:T(1,128)}, u32[]{:S(2)}) copy-start(s32[256,1]{0,1:T(1,128)} %param.11) | copy-start | bytes 3076
  5.5 0.7 %copy-start.5 = (s32[24]{0:T(128)S(1)}, s32[24]{0:T(128)}, u32[]{:S(2)}) copy-start(s32[24]{0:T(128)} %agg_ref.1) | copy-start | bytes 292

commit v3 on v2

--- a/solution.py
+++ b/solution.py
@@ -17,6 +17,8 @@
 COLS = KC * BS
 HALF = COLS // 2
 KT = 7
+SKEW = 25
+TOGETHER = 4
 DIMS = (8, 4, 4)
 MESH = pl.DeviceIdType.MESH
 BF16 = jnp.bfloat16
@@ -37,13 +39,13 @@
     low = low_lanes()
     for half in range(2):
         for t in range(32):
-            stage[half, pl.ds(t * 32, FB), :] = a_ref[
+            stage[half, pl.ds(t * SKEW, FB), :] = a_ref[
                 jnp.minimum(2 * g + half, KA - 1), :, pl.ds(t * 128, 128)
             ].astype(F32)
     column = pl.ds(pl.multiple_of(g * 128, 128), 128)
     for f in range(FB):
-        one = stage[0, pl.ds(f, 32, stride=32), :]
-        two = stage[1, pl.ds(f, 32, stride=32), :]
+        one = stage[0, pl.ds(f, 32, stride=SKEW), :]
+        two = stage[1, pl.ds(f, 32, stride=SKEW), :]
         top, bottom = fold_blocks(one, two, low)
         left[f, pl.ds(0, 32), column] = top.astype(BF16)
         left[f, pl.ds(32, 32), column] = bottom.astype(BF16)
@@ -52,9 +54,9 @@
 def relay_p(w, keep, praw, stage, nat, window, qperm):
     low = low_lanes()
     for t in range(32):
-        stage[0, pl.ds(t * 32, FB), :] = praw[w, :, pl.ds(t * 128, 128)].astype(F32)
+        stage[0, pl.ds(t * SKEW, FB), :] = praw[w, :, pl.ds(t * 128, 128)].astype(F32)
     for b in range(FB):
-        one = stage[0, pl.ds(b, 32, stride=32), :]
+        one = stage[0, pl.ds(b, 32, stride=SKEW), :]
         top, bottom = fold_blocks(one, one, low)
         if keep:
             qperm[pl.ds(b * BS, 32), :] = top
@@ -64,10 +66,15 @@
         window[w * FB + b] = nat[b % 4].astype(BF16)
 
 
-def fill_masks(masks):
-    column_slot = lax.broadcasted_iota(jnp.int32, (16, COLS), 1) // BS
+def fill_masks(slot_mask, side_mask):
+    column_slot = lax.broadcasted_iota(jnp.int32, (16, HALF), 1) // BS
+    first = lax.broadcasted_iota(jnp.int32, (16, 128), 1) < BS
     for s in range(KC):
-        masks[s] = jnp.where(column_slot == s, 1.0, 0.0).astype(BF16)
+        slot_mask[s] = jnp.where(column_slot == s % 4, 1.0, 0.0).astype(BF16)
+        for t in range(KC):
+            below = jnp.where(first, 1.0 - s // 4, 1.0 - t // 4)
+            side_mask[KC * s + t, :, 0:128] = below.astype(BF16)
+            side_mask[KC * s + t, :, 128:256] = (1.0 - below).astype(BF16)
 
 
 def fill_onehot(side, half, owner_ref, onehot):
@@ -105,24 +112,46 @@
             ).astype(BF16)
 
 
-def fine_row(f, h, base, cols_ref, slots_ref, left, window, masks, summed):
-    acc = jnp.zeros((BS, HALF), F32)
+def tall(mask):
+    return jnp.concatenate([mask] * (BS // 16), axis=0)
+
+
+def positions(f, kk, base, cols_ref, slots_ref, left, window, slot_mask, side_mask):
+    blocks, low, high = [], [], []
+    for k in (4 * kk, 4 * kk + 2):
+        slots = [slots_ref[f, min(k + i, KA - 1)] for i in range(2)]
+        for i in range(2):
+            if k + i < KA:
+                block = window[jnp.clip(cols_ref[f, k + i] - base, 0, 3 * FB - 1)]
+                keep = tall(slot_mask[slots[i]])
+                blocks.append(jnp.concatenate([block, block], axis=1) * keep)
+            else:
+                blocks.append(jnp.zeros((BS, HALF), BF16))
+        pair = left[f, :, pl.ds(k * BS, 128)]
+        keep = side_mask[slots[0] * KC + slots[1]]
+        low.append(pair * tall(keep[:, 0:128]))
+        high.append(pair * tall(keep[:, 128:256]))
+    rows = [jnp.concatenate(low, axis=1), jnp.concatenate(high, axis=1)]
+    return jnp.dot(
+        jnp.concatenate(rows, axis=0),
+        jnp.concatenate(blocks, axis=0),
+        preferred_element_type=F32,
+    )
+
+
+def fine_rows(g, base, cols_ref, slots_ref, left, window, slot_mask, side_mask, summed):
+    total = [None] * TOGETHER
     for kk in range(KT):
-        rows = []
-        for k in range(4 * kk, 4 * kk + 4):
-            if k < KA:
-                block = window[jnp.clip(cols_ref[f, k] - base, 0, 3 * FB - 1)]
-                keep = masks[slots_ref[f, k], :, pl.ds(h * HALF, HALF)]
-                keep = jnp.concatenate([keep] * 4, axis=0)
-                rows.append(jnp.concatenate([block, block], axis=1) * keep)
-            else:
-                rows.append(jnp.zeros((BS, HALF), BF16))
-        acc += jnp.dot(
-            left[f, :, pl.ds(kk * 256, 256)],
-            jnp.concatenate(rows, axis=0),
-            preferred_element_type=F32,
-        )
-    summed[pl.ds(pl.multiple_of(f * BS, BS), BS), pl.ds(h * HALF, HALF)] = acc.astype(BF16)
+        for i in range(TOGETHER):
+            f = g * TOGETHER + i
+            term = positions(
+                f, kk, base, cols_ref, slots_ref, left, window, slot_mask, side_mask
+            )
+            total[i] = term if kk == 0 else total[i] + term
+    for i in range(TOGETHER):
+        rows = pl.ds(pl.multiple_of((g * TOGETHER + i) * BS, BS), BS)
+        summed[rows, 0:HALF] = total[i][0:BS].astype(BF16)
+        summed[rows, HALF:COLS] = total[i][BS:].astype(BF16)
 
 
 def place(half, onehot, part, theirs, outbox):
@@ -141,19 +170,24 @@
 def kernel(
     dims,
     a_hbm,
+    cols_hbm,
+    slots_hbm,
+    prolong_hbm,
+    agg_hbm,
+    owner_hbm,
+    out_ref,
     cols_ref,
     slots_ref,
-    prolong_hbm,
     agg_ref,
     owner_ref,
-    out_ref,
     a_ref,
     praw,
     stage,
     nat,
     left,
     window,
-    masks,
+    slot_mask,
+    side_mask,
     qperm,
     turned,
     summed,
@@ -163,6 +197,7 @@
     outbox,
     a_sem,
     p_sem,
+    small_sem,
     near_send,
     near_recv,
     pair_send,
@@ -190,6 +225,19 @@
         fetches.append(pltpu.make_async_copy(a_hbm.at[span], a_ref.at[span], a_sem.at[i]))
     own = pltpu.make_async_copy(prolong_hbm, praw.at[1], p_sem)
     own.start()
+    small = [
+        pltpu.make_async_copy(src, dst, small_sem.at[i])
+        for i, (src, dst) in enumerate(
+            [
+                (owner_hbm, owner_ref),
+                (agg_hbm, agg_ref),
+                (cols_hbm, cols_ref),
+                (slots_hbm, slots_ref),
+            ]
+        )
+    ]
+    for copy in small:
+        copy.start()
     for fetch in fetches:
         fetch.start()
 
@@ -225,9 +273,11 @@
         pl.semaphore_signal(y_sem, inc=1, device_id=(c, core), device_id_type=MESH)
 
     side = (chip // half + core) % 2
-    fill_masks(masks)
+    fill_masks(slot_mask, side_mask)
+    small[0].wait()
     fill_onehot(side, half, owner_ref, onehot)
     relay_p(1, True, praw, stage, nat, window, qperm)
+    small[1].wait()
     fill_turned(chip, agg_ref, qperm, turned)
 
     for i in range(KT):
@@ -248,15 +298,17 @@
     to_beyond.wait_recv()
     relay_p(2 * core, False, praw, stage, nat, window, qperm)
 
+    small[2].wait()
+    small[3].wait()
     base = (chip * 2 + core - 1) * FB
+
+    def rows_step(g, carry):
+        fine_rows(g, base, cols_ref, slots_ref, left, window, slot_mask, side_mask, summed)
+        return carry
+
+    lax.fori_loop(0, FB // TOGETHER, rows_step, 0)
     pair_copies = []
     for h in range(2):
-
-        def row(f, carry):
-            fine_row(f, h, base, cols_ref, slots_ref, left, window, masks, summed)
-            return carry
-
-        lax.fori_loop(0, FB, row, 0)
         part[h] = jnp.dot(
             turned[...], summed[:, pl.ds(h * HALF, HALF)], preferred_element_type=F32
         )
@@ -329,23 +381,27 @@
 def shards(dims, a_blocks, a_cols, slots, prolong, aggregate, owner):
     chips = dims[0] * dims[1] * dims[2]
     half = chips // 2
-    anywhere = pl.BlockSpec(memory_space=pl.ANY)
+    hbm = pl.BlockSpec(memory_space=pltpu.HBM)
     vmem = pl.BlockSpec(memory_space=pltpu.VMEM)
-    smem = pl.BlockSpec(memory_space=pltpu.SMEM)
     dma = pltpu.SemaphoreType.DMA
     arrived = pl.pallas_call(
         functools.partial(kernel, dims),
         out_shape=jax.ShapeDtypeStruct((chips, 16, 128), BF16),
-        in_specs=[anywhere, smem, smem, anywhere, smem, vmem],
+        in_specs=[hbm] * 6,
         out_specs=vmem,
         scratch_shapes=[
+            pltpu.SMEM((FB, KA), jnp.int32),
+            pltpu.SMEM((FB, KA), jnp.int32),
+            pltpu.SMEM((FB,), jnp.int32),
+            pltpu.VMEM((1, ROWS), jnp.int32),
             pltpu.VMEM((KA, FB, BS * BS), BF16),
             pltpu.VMEM((3, FB, BS * BS), BF16),
             pltpu.VMEM((2, 32 * 32, 128), F32),
             pltpu.VMEM((4, BS, 128), F32),
             pltpu.VMEM((FB, BS, KT * 256), BF16),
             pltpu.VMEM((3 * FB, BS, 128), BF16),
-            pltpu.VMEM((KC, 16, COLS), BF16),
+            pltpu.VMEM((KC, 16, HALF), BF16),
+            pltpu.VMEM((KC * KC, 16, HALF), BF16),
             pltpu.VMEM((FB * BS, 128), F32),
             pltpu.VMEM((ROWS, FB * BS), BF16),
             pltpu.VMEM((FB * BS, COLS), BF16),
@@ -355,6 +411,7 @@
             pltpu.VMEM((half, 16, 128), BF16),
             dma((KT,)),
             dma,
+            dma((4,)),
             dma((2,)),
             dma((2,)),
             dma((2,)),
@@ -368,7 +425,7 @@
             pltpu.SemaphoreType.REGULAR,
         ],
         compiler_params=pltpu.CompilerParams(
-            collective_id=0, has_side_effects=True, vmem_limit_bytes=48 * 1024 * 1024
+            collective_id=0, has_side_effects=True, vmem_limit_bytes=60 * 1024 * 1024
         ),
     )(
         jnp.transpose(a_blocks, (1, 0, 2)),

time: 59.2 us -> 37.4 us (0.63)
  Pallas kernels: 51.7 us -> 35.2 us
  local copies, waits for them, and re-layouts: 6.18 us -> 0 us
  other arithmetic: 1.05 us -> 2.09 us
    pallas_call x1, Pallas kernels: 51.7 us -> 35.2 us  [shards(): pl.pallas_call(functools.partial(kernel, dims), out_shape=jax.ShapeDtypeS...]
    unnamed x12 -> x0, local copies, waits for them, and re-layouts: 6.18 us -> none
    unnamed x1, other arithmetic: 1.05 us -> 2.09 us
where the time goes in v3:
time: 37.4 us; the launch traced here: 37.3 us
  Pallas kernels  35.2 us (94%)
  other arithmetic  2.09 us (6%)
    pallas_call x1, Pallas kernels, shards(): pl.pallas_call(functools.partial(kernel, dims), out_shape=jax.ShapeDtypeS...  35.2 us
    unnamed x1, other arithmetic  2.09 us

profile of v3, /device:TPU:33, one launch (start us, length us, event | category | flops | bytes accessed | tf_op | source)
XLA Modules:
  0.0 37.3 jit_solution(5897275131735622075)
XLA Ops:
  0.0 35.2 %shard_map.64 = bf16[128,16,128]{2,1,0:T(8,128)(2,1)} custom-call(bf16[27,24,4096]{2,1,0:T(8,128)(2,1)} %bitcast.10, s32[24,27]{1,0:T(8,128)} %cols_hbm.1, s32[24,27]{1,0:T(8,128)} %slots_hbm.1, bf16[24,4096]{1,0:T(8,128)(2,1)} %prolong_hbm.1, s32[24]{0:T(128)} %agg_hbm.1, s32[1,256]{1,0:T(1,128)} %bitcast.12), custom_call_target="tpu_custom_call" | custom-call | tf_op jit(solution)/shard_map/pallas_call | solution.py:387
  35.2 2.1 %convert.6 = f32[128,16,128]{2,1,0:T(8,128)} convert(bf16[128,16,128]{2,1,0:T(8,128)(2,1)} %shard_map.64) | non-fusion elementwise | flops 262144 | bytes 1572864

commit v4 on v3

--- a/solution.py
+++ b/solution.py
@@ -18,6 +18,8 @@
 HALF = COLS // 2
 KT = 7
 SKEW = 25
+PIECES = 2
+SENDS = 32
 TOGETHER = 4
 DIMS = (8, 4, 4)
 MESH = pl.DeviceIdType.MESH
@@ -77,7 +79,23 @@
             side_mask[KC * s + t, :, 128:256] = (1.0 - below).astype(BF16)
 
 
-def fill_onehot(side, half, owner_ref, onehot):
+def spread(i, n):
+    return n // 2 + (i + 1) // 2 * (1 - 2 * (i % 2))
+
+
+def plane_order(dims, z):
+    nz, nx, ny = dims
+    return [(z + spread(i, nz)) % nz * (nx * ny) for i in range(nz)]
+
+
+def column_order(i, dims, x, y):
+    nz, nx, ny = dims
+    return (x + spread(i // ny, nx)) % nx * ny + (y + spread(i % ny, ny)) % ny
+
+
+def fill_onehot(dims, place_of, owner_ref, onehot):
+    nz, nx, ny = dims
+    z, x, y = place_of
     owner_row = jnp.broadcast_to(owner_ref[...].astype(F32), (128, ROWS))
     owners = jnp.transpose(owner_row)
     target = jnp.where(
@@ -92,12 +110,19 @@
     before = jnp.dot(earlier, target.astype(BF16), preferred_element_type=F32)
     rank = jnp.sum(before * target, axis=1, keepdims=True)
     key_row = jnp.transpose(owners * MOST + rank)[0:1, :]
-    n = min(256, half * 16)
-    row_id = lax.broadcasted_iota(jnp.int32, (n, ROWS), 0)
-    for i in range(half * 16 // n):
-        rid = row_id + i * n
-        code = (side * half + rid // 16) * MOST + rid % MOST
-        onehot[pl.ds(i * n, n), :] = jnp.where(code.astype(F32) == key_row, 1.0, 0.0).astype(BF16)
+    slot = lax.broadcasted_iota(jnp.int32, (16, ROWS), 0) % MOST
+    upper = lax.broadcasted_iota(jnp.int32, (16, ROWS), 0) // 8
+    planes = plane_order(dims, z)
+
+    def column(i, carry):
+        there = column_order(i, dims, x, y)
+        for u in range(0, nz, 2):
+            code = slot + (planes[u] + there) * MOST + upper * ((planes[u + 1] - planes[u]) * MOST)
+            rows = pl.ds(pl.multiple_of((i * nz + u) * 8, 16), 16)
+            onehot[rows, :] = jnp.where(code.astype(F32) == key_row, 1.0, 0.0).astype(BF16)
+        return carry
+
+    lax.fori_loop(0, nx * ny, column, 0)
 
 
 def fill_turned(chip, agg_ref, qperm, turned):
@@ -154,17 +179,12 @@
         summed[rows, HALF:COLS] = total[i][BS:].astype(BF16)
 
 
-def place(half, onehot, part, theirs, outbox):
-    whole = jnp.concatenate([(part[h] + theirs[h]).astype(BF16) for h in range(2)], axis=1)
-    n = min(256, half * 16)
-    group = (lax.broadcasted_iota(jnp.int32, (n, 128), 0) // MOST) % 4
-    for i in range(half * 16 // n):
-        placed = jnp.dot(onehot[pl.ds(i * n, n), :], whole, preferred_element_type=F32)
-        value = placed[:, 384:512]
-        for b in range(3):
-            value = jnp.where(group == b, placed[:, b * 128 : (b + 1) * 128], value)
-        for j in range(n // 16):
-            outbox[i * (n // 16) + j] = value[j * 16 : (j + 1) * 16].astype(BF16)
+def place(i, n, whole, onehot, outbox):
+    first = (lax.broadcasted_iota(jnp.int32, (8 * n, 128), 0) // MOST) % 2 == 0
+    placed = jnp.dot(onehot[pl.ds(i * 8 * n, 8 * n), :], whole, preferred_element_type=F32)
+    value = jnp.where(first, placed[:, 0:128], placed[:, 128:256])
+    for j in range(n):
+        outbox[i * n + j] = value[j * 8 : (j + 1) * 8].astype(BF16)
 
 
 def kernel(
@@ -203,7 +223,6 @@
     pair_send,
     pair_recv,
     out_send,
-    one_send,
     out_recv,
     fwd_send,
     fwd_recv,
@@ -212,7 +231,7 @@
 ):
     nz, nx, ny = dims
     chips = nz * nx * ny
-    half = chips // 2
+    plane = nx * ny
     chip = lax.axis_index("rows")
     core = lax.axis_index("pair")
     other = 1 - core
@@ -248,11 +267,10 @@
     met = [(chip, other), (beyond, other)] + [(c, core) for c in y_ring + x_ring + z_ring]
     for device in met:
         pl.semaphore_signal(barrier, inc=1, device_id=device, device_id_type=MESH)
-    own.wait()
     pl.semaphore_wait(barrier, len(met))
 
     to_partner = pltpu.make_async_remote_copy(
-        src_ref=praw.at[1],
+        src_ref=prolong_hbm,
         dst_ref=praw.at[2 * core],
         send_sem=near_send.at[0],
         recv_sem=near_recv.at[0],
@@ -260,7 +278,7 @@
         device_id_type=MESH,
     )
     to_beyond = pltpu.make_async_remote_copy(
-        src_ref=praw.at[1],
+        src_ref=prolong_hbm,
         dst_ref=praw.at[2 * other],
         send_sem=near_send.at[1],
         recv_sem=near_recv.at[1],
@@ -272,10 +290,10 @@
     for c in y_ring:
         pl.semaphore_signal(y_sem, inc=1, device_id=(c, core), device_id_type=MESH)
 
-    side = (chip // half + core) % 2
     fill_masks(slot_mask, side_mask)
     small[0].wait()
-    fill_onehot(side, half, owner_ref, onehot)
+    fill_onehot(dims, (z, x, y), owner_ref, onehot)
+    own.wait()
     relay_p(1, True, praw, stage, nat, window, qperm)
     small[1].wait()
     fill_turned(chip, agg_ref, qperm, turned)
@@ -307,86 +325,95 @@
         return carry
 
     lax.fori_loop(0, FB // TOGETHER, rows_step, 0)
-    pair_copies = []
-    for h in range(2):
-        part[h] = jnp.dot(
-            turned[...], summed[:, pl.ds(h * HALF, HALF)], preferred_element_type=F32
-        )
-        copy = pltpu.make_async_remote_copy(
-            src_ref=part.at[h],
-            dst_ref=theirs.at[h],
-            send_sem=pair_send.at[h],
-            recv_sem=pair_recv.at[h],
+    exchanges = []
+    for i, h in enumerate((other, core)):
+        for j in range(PIECES):
+            rows = pl.ds(j * (ROWS // PIECES), ROWS // PIECES)
+            part[i, rows, :] = jnp.dot(
+                turned[rows, :],
+                summed[:, pl.ds(pl.multiple_of(h * HALF, HALF), HALF)],
+                preferred_element_type=F32,
+            )
+            if i == 0:
+                exchange = pltpu.make_async_remote_copy(
+                    src_ref=part.at[0, rows],
+                    dst_ref=theirs.at[rows],
+                    send_sem=pair_send.at[j],
+                    recv_sem=pair_recv.at[j],
+                    device_id=(chip, other),
+                    device_id_type=MESH,
+                )
+                exchange.start()
+                exchanges.append(exchange)
+
+    planes = plane_order(dims, z)
+
+    def column(i, carry):
+        there = column_order(i, dims, x, y)
+        for u in range(nz):
+
+            def send(u=u):
+                pltpu.make_async_remote_copy(
+                    src_ref=outbox.at[i * nz + u],
+                    dst_ref=out_ref.at[chip, core],
+                    send_sem=out_send,
+                    recv_sem=out_recv.at[z],
+                    device_id=(planes[u] + there, core),
+                    device_id_type=MESH,
+                ).start()
+
+            if u < nz - 1:
+                send()
+            else:
+                pl.when(i < plane - 1)(send)
+        return carry
+
+    pl.semaphore_wait(x_sem, nx - 1)
+    for exchange in exchanges:
+        exchange.wait_recv()
+    whole = (part[1] + theirs[...]).astype(BF16)
+    n = min(SENDS, chips)
+    for i in range(chips // n):
+        place(i, n, whole, onehot, outbox)
+        lax.fori_loop(i * n // nz, (i + 1) * n // nz, column, 0)
+    last = chips - 1
+    pltpu.make_async_copy(outbox.at[last], out_ref.at[chip, core], out_recv.at[z]).start()
+
+    forwards = []
+    for i in range(nz):
+        there = (z + i) % nz
+        arrived = out_ref.at[pl.ds(there * plane, plane), core]
+        pltpu.make_async_copy(arrived, arrived, out_recv.at[there]).wait()
+        forward = pltpu.make_async_remote_copy(
+            src_ref=arrived,
+            dst_ref=arrived,
+            send_sem=fwd_send.at[there],
+            recv_sem=fwd_recv.at[there],
             device_id=(chip, other),
             device_id_type=MESH,
         )
-        copy.start()
-        pair_copies.append(copy)
-
-    pl.semaphore_wait(x_sem, nx - 1)
-    for copy in pair_copies:
-        copy.wait()
-    place(half, onehot, part, theirs, outbox)
-
-    mine = chip % half
-
-    def send(i, sem):
-        there = (mine + i) % half
-        return pltpu.make_async_remote_copy(
-            src_ref=outbox.at[there],
-            dst_ref=out_ref.at[chip],
-            send_sem=sem,
-            recv_sem=out_recv,
-            device_id=(side * half + there, core),
-            device_id_type=MESH,
-        )
-
-    def send_loop(i, carry):
-        send(i, out_send).start()
-        return carry
-
-    lax.fori_loop(1, half, send_loop, 0)
-
-    @pl.when(core == 0)
-    def _():
-        pltpu.make_async_copy(outbox.at[mine], out_ref.at[chip], out_recv).start()
-
-    @pl.when(core == 1)
-    def _():
-        send(0, one_send).start()
-
-    arrived = out_ref.at[pl.ds(side * half, half)]
-    pltpu.make_async_copy(arrived, arrived, out_recv).wait()
-    forward = pltpu.make_async_remote_copy(
-        src_ref=arrived,
-        dst_ref=arrived,
-        send_sem=fwd_send,
-        recv_sem=fwd_recv,
-        device_id=(chip, other),
-        device_id_type=MESH,
-    )
-    forward.start()
-    sent = outbox.at[pl.ds(0, half - 1)]
+        forward.start()
+        forwards.append(forward)
+    sent = outbox.at[pl.ds(0, chips - 1)]
     pltpu.make_async_copy(sent, sent, out_send).wait()
-
-    @pl.when(core == 1)
-    def _():
-        send(0, one_send).wait_send()
-
     to_partner.wait_send()
     to_beyond.wait_send()
-    forward.wait()
+    for exchange in exchanges:
+        exchange.wait_send()
+    for i in range(nz):
+        forwards[i].wait_send()
+        theirs_there = out_ref.at[pl.ds((z + i) % nz * plane, plane), other]
+        pltpu.make_async_copy(theirs_there, theirs_there, fwd_recv.at[(z + i) % nz]).wait()
 
 
 def shards(dims, a_blocks, a_cols, slots, prolong, aggregate, owner):
     chips = dims[0] * dims[1] * dims[2]
-    half = chips // 2
     hbm = pl.BlockSpec(memory_space=pltpu.HBM)
     vmem = pl.BlockSpec(memory_space=pltpu.VMEM)
     dma = pltpu.SemaphoreType.DMA
     arrived = pl.pallas_call(
         functools.partial(kernel, dims),
-        out_shape=jax.ShapeDtypeStruct((chips, 16, 128), BF16),
+        out_shape=jax.ShapeDtypeStruct((chips, 2, 8, 128), BF16),
         in_specs=[hbm] * 6,
         out_specs=vmem,
         scratch_shapes=[
@@ -405,35 +432,39 @@
             pltpu.VMEM((FB * BS, 128), F32),
             pltpu.VMEM((ROWS, FB * BS), BF16),
             pltpu.VMEM((FB * BS, COLS), BF16),
-            pltpu.VMEM((half * 16, ROWS), BF16),
+            pltpu.VMEM((chips * 8, ROWS), BF16),
             pltpu.VMEM((2, ROWS, HALF), F32),
-            pltpu.VMEM((2, ROWS, HALF), F32),
-            pltpu.VMEM((half, 16, 128), BF16),
+            pltpu.VMEM((ROWS, HALF), F32),
+            pltpu.VMEM((chips, 8, 128), BF16),
             dma((KT,)),
             dma,
             dma((4,)),
             dma((2,)),
             dma((2,)),
-            dma((2,)),
-            dma((2,)),
+            dma((PIECES,)),
+            dma((PIECES,)),
             dma,
-            dma,
-            dma,
-            dma,
-            dma,
+            dma((dims[0],)),
+            dma((dims[0],)),
+            dma((dims[0],)),
             pltpu.SemaphoreType.REGULAR,
             pltpu.SemaphoreType.REGULAR,
         ],
         compiler_params=pltpu.CompilerParams(
-            collective_id=0, has_side_effects=True, vmem_limit_bytes=60 * 1024 * 1024
+            collective_id=0, has_side_effects=True, vmem_limit_bytes=48 * 1024 * 1024
         ),
     )(
-        jnp.transpose(a_blocks, (1, 0, 2)),
-        a_cols,
-        slots,
-        prolong,
-        aggregate,
-        owner.reshape(1, ROWS),
+        *[
+            pltpu.with_memory_space_constraint(x, pltpu.HBM)
+            for x in (
+                jnp.transpose(a_blocks, (1, 0, 2)),
+                a_cols,
+                slots,
+                prolong,
+                aggregate,
+                owner.reshape(1, ROWS),
+            )
+        ]
     )
     rows = arrived.reshape(chips, 4, MOST, 128).astype(F32)
     return jnp.transpose(rows, (0, 2, 1, 3)).reshape(1, chips, MOST, COLS)

time: 37.4 us -> 35.4 us (0.947)
  the two profiles are of different devices: /device:TPU:33 before, /device:TPU:1 now
where the time goes in v4:
time: 35.4 us; the launch traced here: 35.3 us
  Pallas kernels  34.2 us (97%)
  other arithmetic  1.05 us (3%)
    pallas_call x1, Pallas kernels, shards(): pl.pallas_call(functools.partial(kernel, dims), out_shape=jax.ShapeDtypeS...  34.2 us
    unnamed x1, other arithmetic  1.05 us

profile of v4, /device:TPU:1, one launch (start us, length us, event | category | flops | bytes accessed | tf_op | source)
XLA Modules:
  0.0 35.3 jit_solution(12327473272216335552)
XLA Ops:
  0.0 34.2 %shard_map.64 = bf16[128,2,8,128]{3,2,1,0:T(8,128)(2,1)S(1)} custom-call(bf16[27,24,4096]{2,1,0:T(8,128)(2,1)} %bitcast.10, s32[24,27]{1,0:T(8,128)} %cols_hbm.1, s32[24,27]{1,0:T(8,128)} %slots_hbm.1, bf16[24,4096]{1,0:T(8,128)(2,1)} %prolong_hbm.1, s32[24]{0:T(128)} %agg_hbm.1, s32[1,256]{1,0:T(1,128)} %bitcast.12), custom_call_target="tpu_custom_call" | custom-call | tf_op jit(solution)/shard_map/pallas_call | solution.py:414
  34.3 1.0 %convert.6 = f32[128,2,8,128]{3,2,1,0:T(8,128)} convert(bf16[128,2,8,128]{3,2,1,0:T(8,128)(2,1)S(1)} %shard_map.64) | non-fusion elementwise | flops 262144 | bytes 1572864

commit v5 on v4

--- a/solution.py
+++ b/solution.py
@@ -20,7 +20,7 @@
 SKEW = 25
 PIECES = 2
 SENDS = 32
-TOGETHER = 4
+TOGETHER = 6
 DIMS = (8, 4, 4)
 MESH = pl.DeviceIdType.MESH
 BF16 = jnp.bfloat16
@@ -83,9 +83,11 @@
     return n // 2 + (i + 1) // 2 * (1 - 2 * (i % 2))
 
 
-def plane_order(dims, z):
+def plane_order(dims, z, own):
     nz, nx, ny = dims
-    return [(z + spread(i, nz)) % nz * (nx * ny) for i in range(nz)]
+    half = nz // 2
+    side = (z // half + 1 - own) % 2
+    return [(side * half + (z + own + i) % half) * (nx * ny) for i in range(half)]
 
 
 def column_order(i, dims, x, y):
@@ -112,17 +114,19 @@
     key_row = jnp.transpose(owners * MOST + rank)[0:1, :]
     slot = lax.broadcasted_iota(jnp.int32, (16, ROWS), 0) % MOST
     upper = lax.broadcasted_iota(jnp.int32, (16, ROWS), 0) // 8
-    planes = plane_order(dims, z)
-
-    def column(i, carry):
+    half = nz // 2
+
+    def column(own, planes, i, carry):
         there = column_order(i, dims, x, y)
-        for u in range(0, nz, 2):
+        for u in range(0, half, 2):
             code = slot + (planes[u] + there) * MOST + upper * ((planes[u + 1] - planes[u]) * MOST)
-            rows = pl.ds(pl.multiple_of((i * nz + u) * 8, 16), 16)
+            rows = pl.ds(pl.multiple_of(((own * nx * ny + i) * half + u) * 8, 16), 16)
             onehot[rows, :] = jnp.where(code.astype(F32) == key_row, 1.0, 0.0).astype(BF16)
         return carry
 
-    lax.fori_loop(0, nx * ny, column, 0)
+    for own in range(2):
+        planes = plane_order(dims, z, own)
+        lax.fori_loop(0, nx * ny, functools.partial(column, own, planes), 0)
 
 
 def fill_turned(chip, agg_ref, qperm, turned):
@@ -226,8 +230,7 @@
     out_recv,
     fwd_send,
     fwd_recv,
-    y_sem,
-    x_sem,
+    ring_sem,
 ):
     nz, nx, ny = dims
     chips = nz * nx * ny
@@ -236,8 +239,25 @@
     core = lax.axis_index("pair")
     other = 1 - core
     z, x, y = chip // (nx * ny), (chip // ny) % nx, chip % ny
-    beyond = (chip + chips - 1 + 2 * core) % chips
-
+    beyond = chip - 1 + 2 * core
+    has_beyond = jnp.logical_and(beyond >= 0, beyond < chips)
+
+    z_ring = [((z + i) % nz * nx + x) * ny + y for i in range(1, nz)]
+    x_ring = [(z * nx + (x + i) % nx) * ny + y for i in range(1, nx)]
+    y_ring = [(z * nx + x) * ny + (y + i) % ny for i in range(1, ny)]
+
+    def signal_ring(sem, ring):
+        for there in ring:
+            pl.semaphore_signal(sem, inc=1, device_id=(there, core), device_id_type=MESH)
+
+    barrier = pltpu.get_barrier_semaphore()
+    pl.semaphore_signal(barrier, inc=1, device_id=(chip, other), device_id_type=MESH)
+
+    @pl.when(has_beyond)
+    def _():
+        pl.semaphore_signal(barrier, inc=1, device_id=(beyond, other), device_id_type=MESH)
+
+    signal_ring(barrier, y_ring + x_ring + z_ring)
     fetches = []
     for i in range(KT):
         span = pl.ds(4 * i, min(4, KA - 4 * i))
@@ -257,20 +277,16 @@
     ]
     for copy in small:
         copy.start()
-    for fetch in fetches:
-        fetch.start()
-
-    y_ring = [(z * nx + x) * ny + (y + i) % ny for i in range(1, ny)]
-    x_ring = [(z * nx + (x + i) % nx) * ny + y for i in range(1, nx)]
-    z_ring = [(((z + i) % nz) * nx + x) * ny + y for i in range(1, nz)]
-    barrier = pltpu.get_barrier_semaphore()
-    met = [(chip, other), (beyond, other)] + [(c, core) for c in y_ring + x_ring + z_ring]
-    for device in met:
-        pl.semaphore_signal(barrier, inc=1, device_id=device, device_id_type=MESH)
-    pl.semaphore_wait(barrier, len(met))
-
+
+    fill_masks(slot_mask, side_mask)
+    pl.semaphore_wait(
+        barrier,
+        1 + has_beyond.astype(jnp.int32) + nz + nx + ny - 3,
+    )
+
+    own.wait()
     to_partner = pltpu.make_async_remote_copy(
-        src_ref=prolong_hbm,
+        src_ref=praw.at[1],
         dst_ref=praw.at[2 * core],
         send_sem=near_send.at[0],
         recv_sem=near_recv.at[0],
@@ -278,22 +294,19 @@
         device_id_type=MESH,
     )
     to_beyond = pltpu.make_async_remote_copy(
-        src_ref=prolong_hbm,
+        src_ref=praw.at[1],
         dst_ref=praw.at[2 * other],
         send_sem=near_send.at[1],
         recv_sem=near_recv.at[1],
         device_id=(beyond, other),
         device_id_type=MESH,
     )
-    to_beyond.start()
+    pl.when(has_beyond)(to_beyond.start)
     to_partner.start()
-    for c in y_ring:
-        pl.semaphore_signal(y_sem, inc=1, device_id=(c, core), device_id_type=MESH)
-
-    fill_masks(slot_mask, side_mask)
-    small[0].wait()
-    fill_onehot(dims, (z, x, y), owner_ref, onehot)
-    own.wait()
+    for fetch in fetches:
+        fetch.start()
+    signal_ring(ring_sem.at[0], y_ring)
+
     relay_p(1, True, praw, stage, nat, window, qperm)
     small[1].wait()
     fill_turned(chip, agg_ref, qperm, turned)
@@ -307,13 +320,11 @@
 
         lax.fori_loop(2 * i, 2 * i + 2, relay, 0)
 
-    pl.semaphore_wait(y_sem, ny - 1)
-    for c in x_ring:
-        pl.semaphore_signal(x_sem, inc=1, device_id=(c, core), device_id_type=MESH)
-
+    pl.semaphore_wait(ring_sem.at[0], ny - 1)
+    signal_ring(ring_sem.at[1], x_ring)
     to_partner.wait_recv()
     relay_p(2 * other, False, praw, stage, nat, window, qperm)
-    to_beyond.wait_recv()
+    pl.when(has_beyond)(to_beyond.wait_recv)
     relay_p(2 * core, False, praw, stage, nat, window, qperm)
 
     small[2].wait()
@@ -346,15 +357,15 @@
                 exchange.start()
                 exchanges.append(exchange)
 
-    planes = plane_order(dims, z)
-
-    def column(i, carry):
+    span = nz // 2
+
+    def column(own, planes, i, carry):
         there = column_order(i, dims, x, y)
-        for u in range(nz):
+        for u in range(span):
 
             def send(u=u):
                 pltpu.make_async_remote_copy(
-                    src_ref=outbox.at[i * nz + u],
+                    src_ref=outbox.at[(own * plane + i) * span + u],
                     dst_ref=out_ref.at[chip, core],
                     send_sem=out_send,
                     recv_sem=out_recv.at[z],
@@ -362,20 +373,24 @@
                     device_id_type=MESH,
                 ).start()
 
-            if u < nz - 1:
+            if own == 0 or u < span - 1:
                 send()
             else:
                 pl.when(i < plane - 1)(send)
         return carry
 
-    pl.semaphore_wait(x_sem, nx - 1)
+    small[0].wait()
+    fill_onehot(dims, (z, x, y), owner_ref, onehot)
+    pl.semaphore_wait(ring_sem.at[1], nx - 1)
     for exchange in exchanges:
         exchange.wait_recv()
     whole = (part[1] + theirs[...]).astype(BF16)
     n = min(SENDS, chips)
     for i in range(chips // n):
         place(i, n, whole, onehot, outbox)
-        lax.fori_loop(i * n // nz, (i + 1) * n // nz, column, 0)
+        own, first = divmod(i * n // span, plane)
+        step = functools.partial(column, own, plane_order(dims, z, own))
+        lax.fori_loop(first, first + n // span, step, 0)
     last = chips - 1
     pltpu.make_async_copy(outbox.at[last], out_ref.at[chip, core], out_recv.at[z]).start()
 
@@ -397,7 +412,7 @@
     sent = outbox.at[pl.ds(0, chips - 1)]
     pltpu.make_async_copy(sent, sent, out_send).wait()
     to_partner.wait_send()
-    to_beyond.wait_send()
+    pl.when(has_beyond)(to_beyond.wait_send)
     for exchange in exchanges:
         exchange.wait_send()
     for i in range(nz):
@@ -447,8 +462,7 @@
             dma((dims[0],)),
             dma((dims[0],)),
             dma((dims[0],)),
-            pltpu.SemaphoreType.REGULAR,
-            pltpu.SemaphoreType.REGULAR,
+            pltpu.SemaphoreType.REGULAR((2,)),
         ],
         compiler_params=pltpu.CompilerParams(
             collective_id=0, has_side_effects=True, vmem_limit_bytes=48 * 1024 * 1024

time: 35.4 us -> 34.7 us (0.980)
  Pallas kernels: 34.2 us -> 33.6 us
    pallas_call x1, Pallas kernels: 34.2 us -> 33.6 us  [shards(): pl.pallas_call(functools.partial(kernel, dims), out_shape=jax.ShapeDtypeS...]
where the time goes in v5:
time: 34.7 us; the launch traced here: 34.6 us
  Pallas kernels  33.6 us (97%)
  other arithmetic  1.05 us (3%)
    pallas_call x1, Pallas kernels, shards(): pl.pallas_call(functools.partial(kernel, dims), out_shape=jax.ShapeDtypeS...  33.6 us
    unnamed x1, other arithmetic  1.05 us

profile of v5, /device:TPU:1, one launch (start us, length us, event | category | flops | bytes accessed | tf_op | source)
XLA Modules:
  0.0 34.6 jit_solution(6325970769255440167)
XLA Ops:
  0.0 33.6 %shard_map.64 = bf16[128,2,8,128]{3,2,1,0:T(8,128)(2,1)S(1)} custom-call(bf16[27,24,4096]{2,1,0:T(8,128)(2,1)} %bitcast.10, s32[24,27]{1,0:T(8,128)} %cols_hbm.1, s32[24,27]{1,0:T(8,128)} %slots_hbm.1, bf16[24,4096]{1,0:T(8,128)(2,1)} %prolong_hbm.1, s32[24]{0:T(128)} %agg_hbm.1, s32[1,256]{1,0:T(1,128)} %bitcast.12), custom_call_target="tpu_custom_call" | custom-call | tf_op jit(solution)/shard_map/pallas_call | solution.py:429
  33.6 1.0 %convert.6 = f32[128,2,8,128]{3,2,1,0:T(8,128)} convert(bf16[128,2,8,128]{3,2,1,0:T(8,128)(2,1)S(1)} %shard_map.64) | non-fusion elementwise | flops 262144 | bytes 1572864

commit v6 on v5

--- a/solution.py
+++ b/solution.py
@@ -18,9 +18,9 @@
 HALF = COLS // 2
 KT = 7
 SKEW = 25
-PIECES = 2
+PIECES = 1
 SENDS = 32
-TOGETHER = 6
+TOGETHER = 12
 DIMS = (8, 4, 4)
 MESH = pl.DeviceIdType.MESH
 BF16 = jnp.bfloat16

time: 34.7 us -> 34.3 us (0.988)
  Pallas kernels: 33.6 us -> 33.2 us
    pallas_call x1, Pallas kernels: 33.6 us -> 33.2 us  [shards(): pl.pallas_call(functools.partial(kernel, dims), out_shape=jax.ShapeDtypeS...]
where the time goes in v6:
time: 34.3 us
  Pallas kernels  33.2 us (97%)
  other arithmetic  1.05 us (3%)
    pallas_call x1, Pallas kernels, shards(): pl.pallas_call(functools.partial(kernel, dims), out_shape=jax.ShapeDtypeS...  33.2 us
    unnamed x1, other arithmetic  1.05 us

profile of v6, /device:TPU:1, one launch (start us, length us, event | category | flops | bytes accessed | tf_op | source)
XLA Modules:
  0.0 34.3 jit_solution(14317041120657429701)
XLA Ops:
  0.0 33.2 %shard_map.64 = bf16[128,2,8,128]{3,2,1,0:T(8,128)(2,1)S(1)} custom-call(bf16[27,24,4096]{2,1,0:T(8,128)(2,1)} %bitcast.10, s32[24,27]{1,0:T(8,128)} %cols_hbm.1, s32[24,27]{1,0:T(8,128)} %slots_hbm.1, bf16[24,4096]{1,0:T(8,128)(2,1)} %prolong_hbm.1, s32[24]{0:T(128)} %agg_hbm.1, s32[1,256]{1,0:T(1,128)} %bitcast.12), custom_call_target="tpu_custom_call" | custom-call | tf_op jit(solution)/shard_map/pallas_call | solution.py:429
  33.2 1.0 %convert.6 = f32[128,2,8,128]{3,2,1,0:T(8,128)} convert(bf16[128,2,8,128]{3,2,1,0:T(8,128)(2,1)S(1)} %shard_map.64) | non-fusion elementwise | flops 262144 | bytes 1572864

commit v7 on v6

--- a/solution.py
+++ b/solution.py
@@ -319,11 +319,12 @@
             return carry
 
         lax.fori_loop(2 * i, 2 * i + 2, relay, 0)
+        if i == 4:
+            to_partner.wait_recv()
+            relay_p(2 * other, False, praw, stage, nat, window, qperm)
 
     pl.semaphore_wait(ring_sem.at[0], ny - 1)
     signal_ring(ring_sem.at[1], x_ring)
-    to_partner.wait_recv()
-    relay_p(2 * other, False, praw, stage, nat, window, qperm)
     pl.when(has_beyond)(to_beyond.wait_recv)
     relay_p(2 * core, False, praw, stage, nat, window, qperm)
 

time: 34.3 us -> 34.4 us (level)
  no operation moved by 1% of the time
where the time goes in v7:
time: 34.4 us; the launch traced here: 34.3 us
  Pallas kernels  33.2 us (97%)
  other arithmetic  1.05 us (3%)
    pallas_call x1, Pallas kernels, shards(): pl.pallas_call(functools.partial(kernel, dims), out_shape=jax.ShapeDtypeS...  33.2 us
    unnamed x1, other arithmetic  1.05 us

profile of v7, /device:TPU:1, one launch (start us, length us, event | category | flops | bytes accessed | tf_op | source)
XLA Modules:
  0.0 34.3 jit_solution(2259542604132274119)
XLA Ops:
  0.0 33.2 %shard_map.64 = bf16[128,2,8,128]{3,2,1,0:T(8,128)(2,1)S(1)} custom-call(bf16[27,24,4096]{2,1,0:T(8,128)(2,1)} %bitcast.10, s32[24,27]{1,0:T(8,128)} %cols_hbm.1, s32[24,27]{1,0:T(8,128)} %slots_hbm.1, bf16[24,4096]{1,0:T(8,128)(2,1)} %prolong_hbm.1, s32[24]{0:T(128)} %agg_hbm.1, s32[1,256]{1,0:T(1,128)} %bitcast.12), custom_call_target="tpu_custom_call" | custom-call | tf_op jit(solution)/shard_map/pallas_call | solution.py:430
  33.2 1.0 %convert.6 = f32[128,2,8,128]{3,2,1,0:T(8,128)} convert(bf16[128,2,8,128]{3,2,1,0:T(8,128)(2,1)S(1)} %shard_map.64) | non-fusion elementwise | flops 262144 | bytes 1572864
